TPU v7x, 32 devices: a whole 2x2x4 slice. The times are simulated.
32 devices in a mesh: groups: 2 (over y), chan: 4 (over z), tm: 4 (over x, core).
Axes of the slice: x: 2, y: 2, z: 4, core: 2. Of those that a mesh axis runs over, the one named last changes fastest.
Arguments:
- raw: bfloat16 [8192, 2048], P(('groups', 'chan'), 'tm'), parts along dimension 0, may hold values from -20 to 20
- send_blocks: int32 [4, 4, 4, 1], P('chan', 'tm'), may hold values from 0 to 1, as said below
- pair_count: int32 [4, 4, 4], P('chan', 'tm'), may hold values from 0 to 1, as said below
Outputs:
- xspec: bfloat16 [8, 4, 4, 1, 2, 2, 128, 128], P(('groups', 'chan'), 'tm'), parts along dimension 0
There are 2 independent parts, one for each index of `groups`. A program takes and returns all parts, laid end to end along the dimension named above; an argument that names none is the same for every part. Nothing has to cross between parts.
Inputs may be any that keep to these rules, and one draw needn't show every extreme that they name: Each list send_blocks[p, t, c, :] names 1 distinct local blocks of device (p, t). pair_count[c, t, c] is 0; pair_count[c, t, p] is 1 where p and c differ by one; in every index t of tm some owner has 1 from every other source.
All inputs are finite; a program needn't handle non-finite values.
Results may differ from a plain program's by a relative error of at most 0.0066.
Values may be sent and summed in bfloat16 or wider, within the bound.
A program may use at most 192 MiB of HBM per device.

v0:
```python
import math

import jax
import jax.numpy as jnp
import numpy as np
from jax import lax
from jax.sharding import PartitionSpec as P

BLOCK = 128
NT = 2048
F0 = 128
NBAND = 512
SUBW = 64
RAD = 15


def sinc_value(arg):
    if arg == 0:
        return 1.0
    return math.sin(math.pi * arg) / (math.pi * arg)


def filter_taps():
    low = F0 / NT
    high = (F0 + NBAND) / NT
    taps = []
    for offset in range(-RAD, RAD + 1):
        value = 2.0 * high * sinc_value(2.0 * high * offset) - 2.0 * low * sinc_value(
            2.0 * low * offset
        )
        value = value * (0.5 + 0.5 * math.cos(math.pi * offset / (RAD + 1)))
        taps.append(value)
    return taps


def dft_table():
    samples = np.arange(NT)[:, None]
    freqs = np.arange(F0, F0 + NBAND)[None, :]
    phase = samples * freqs % NT
    angle = 2.0 * np.pi * phase / NT
    return np.concatenate([np.cos(angle), -np.sin(angle)], axis=1)


def band_filter(slab):
    taps = filter_taps()
    signal = slab.astype(jnp.float32)
    total = jnp.zeros(signal.shape, jnp.float32)
    for index in range(2 * RAD + 1):
        total = total + jnp.float32(taps[index]) * jnp.roll(signal, index - RAD, axis=1)
    return total.astype(jnp.bfloat16)


def whiten(spectrum):
    rows = spectrum.shape[0]
    real_part = spectrum[:, :NBAND].reshape(rows, NBAND // SUBW, SUBW)
    imag_part = spectrum[:, NBAND:].reshape(rows, NBAND // SUBW, SUBW)
    power = jnp.mean(real_part * real_part + imag_part * imag_part, axis=2, keepdims=True)
    level = 1.0 / jnp.sqrt(power + 1e-06)
    out = jnp.concatenate(
        [(real_part * level).reshape(rows, NBAND), (imag_part * level).reshape(rows, NBAND)], axis=1
    )
    return out.astype(jnp.bfloat16)


def local(raw, send_blocks, pair_count):
    rows = lax.all_to_all(raw, "tm", split_axis=0, concat_axis=1, tiled=True)
    table = jnp.asarray(dft_table(), dtype=jnp.bfloat16)
    spectrum = jnp.dot(band_filter(rows), table, preferred_element_type=jnp.float32)
    blocks = rows.shape[0] // BLOCK
    whitened = whiten(spectrum).reshape(blocks, BLOCK, 2 * NBAND)
    peers = lax.axis_size("chan")
    width = send_blocks.shape[3]
    every, lists_all = (
        lax.all_gather(whitened, "chan", axis=0, tiled=True),
        lax.all_gather(send_blocks.astype(jnp.bfloat16), "chan", axis=0, tiled=True),
    )
    mine = lax.axis_index("chan")
    column = lax.dynamic_index_in_dim(lists_all[:, 0], mine, axis=1, keepdims=False)
    flat_ids = jnp.arange(peers, dtype=jnp.int32)[:, None] * blocks + column.astype(jnp.int32)
    picked = every[flat_ids]
    turned = jnp.concatenate([whitened[..., NBAND:], -whitened[..., :NBAND]], axis=-1)
    paired = jnp.stack([whitened, turned], axis=1)
    result = jnp.einsum("lrif,pkjf->pklrij", paired, picked, preferred_element_type=jnp.float32)
    result = result * (1.0 / math.sqrt(NBAND))
    live = jnp.arange(width, dtype=jnp.int32)[None, :] < pair_count[0, 0][:, None]
    result = jnp.where(live[:, :, None, None, None, None], result, 0.0)
    return result.astype(jnp.bfloat16)[None, None]


def solution(mesh):
    return jax.shard_map(
        local,
        mesh=mesh,
        in_specs=(P(("groups", "chan"), "tm"), P("chan", "tm", None, None), P("chan", "tm", None)),
        out_specs=P(("groups", "chan"), "tm", None, None, None, None, None, None),
        check_vma=False,
    )
```

profile of v0, /device:TPU:0, one launch (start us, length us, event | category | flops | bytes accessed | tf_op | source)
XLA Modules:
  0.0 150.9 jit_solution(17581047669316288742)
XLA Ops:
  6.5 0.0 all-gather.2.cloned.1.call-start
  6.5 18.7 %all_to_all.13 = bf16[4,256,512]{2,1,0:T(8,128)(2,1)S(1)} all-to-all(bf16[4,256,512]{2,1,0:T(8,128)(2,1)} %bitcast.81), channel_id=1, replica_groups=mesh['groups'=2,'chan'=4,'tm'=4] {'tm'}, dimensions={0} | all-to-all | bytes 2097152 | tf_op jit(solution)/shard_map/all_to_all | solution.py:66
  25.2 1.6 %convert_bitcast_fusion = f32[256,4,512]{2,0,1:T(8,128)} fusion(bf16[4,256,512]{2,1,0:T(8,128)(2,1)S(1)} %all_to_all.13), kind=kLoop, calls=%fused_computation.62 | loop fusion | flops 524288 | bytes 3145728 | tf_op jit(solution)/shard_map/convert_element_type | solution.py:46
  26.8 1.9 %copy.21 = f32[256,4,512]{0,2,1:T(8,128)S(1)} copy(f32[256,4,512]{2,0,1:T(8,128)} %convert_bitcast_fusion) | data formatting | bytes 4194304 | tf_op jit(solution)/shard_map/convert_element_type | solution.py:46
  28.8 2.3 %fusion.76 = (f32[256,2041]{0,1:T(8,128)}, f32[256,2041]{0,1:T(8,128)}) fusion(f32[256,2048]{0,1:T(8,128)S(1)} %bitcast.46), kind=kLoop, calls=%fused_computation.121 | loop fusion | bytes 8359936 | tf_op jit(solution)/shard_map/jit(_roll_static)/slice | solution.py:49
  31.1 2.3 %fusion.78 = (f32[256,2042]{0,1:T(8,128)}, f32[256,2042]{0,1:T(8,128)}) fusion(f32[256,2048]{0,1:T(8,128)S(1)} %bitcast.47), kind=kLoop, calls=%fused_computation.123 | loop fusion | bytes 8364032 | tf_op jit(solution)/shard_map/jit(_roll_static)/slice | solution.py:49
  33.4 2.3 %fusion.80 = (f32[256,2043]{0,1:T(8,128)}, f32[256,2043]{0,1:T(8,128)}) fusion(f32[256,2048]{0,1:T(8,128)S(1)} %bitcast.48), kind=kLoop, calls=%fused_computation.125 | loop fusion | bytes 8368128 | tf_op jit(solution)/shard_map/jit(_roll_static)/slice | solution.py:49
  35.7 2.3 %fusion.82 = (f32[256,2044]{0,1:T(8,128)}, f32[256,2044]{0,1:T(8,128)}) fusion(f32[256,2048]{0,1:T(8,128)S(1)} %bitcast.49), kind=kLoop, calls=%fused_computation.127 | loop fusion | bytes 8372224 | tf_op jit(solution)/shard_map/jit(_roll_static)/slice | solution.py:49
  38.0 2.3 %fusion.84 = (f32[256,2045]{0,1:T(8,128)}, f32[256,2045]{0,1:T(8,128)}) fusion(f32[256,2048]{0,1:T(8,128)S(1)} %bitcast.50), kind=kLoop, calls=%fused_computation.129 | loop fusion | bytes 8376320 | tf_op jit(solution)/shard_map/jit(_roll_static)/slice | solution.py:49
  40.3 2.3 %fusion.86 = (f32[256,2046]{0,1:T(8,128)}, f32[256,2046]{0,1:T(8,128)}) fusion(f32[256,2048]{0,1:T(8,128)S(1)} %bitcast.51), kind=kLoop, calls=%fused_computation.131 | loop fusion | bytes 8380416 | tf_op jit(solution)/shard_map/jit(_roll_static)/slice | solution.py:49
  42.6 2.3 %fusion.88 = (f32[256,2047]{0,1:T(8,128)}, f32[256,2047]{0,1:T(8,128)}) fusion(f32[256,2048]{0,1:T(8,128)S(1)} %bitcast.52), kind=kLoop, calls=%fused_computation.133 | loop fusion | bytes 8384512 | tf_op jit(solution)/shard_map/jit(_roll_static)/slice | solution.py:49
  44.9 2.3 %fusion.62 = (f32[256,2034]{0,1:T(8,128)}, f32[256,2034]{0,1:T(8,128)}) fusion(f32[256,2048]{0,1:T(8,128)S(1)} %bitcast.53), kind=kLoop, calls=%fused_computation.107 | loop fusion | bytes 8331264 | tf_op jit(solution)/shard_map/jit(_roll_static)/slice | solution.py:49
  47.2 2.3 %fusion.64 = (f32[256,2035]{0,1:T(8,128)}, f32[256,2035]{0,1:T(8,128)}) fusion(f32[256,2048]{0,1:T(8,128)S(1)} %bitcast.54), kind=kLoop, calls=%fused_computation.109 | loop fusion | bytes 8335360 | tf_op jit(solution)/shard_map/jit(_roll_static)/slice | solution.py:49
  49.5 2.3 %fusion.66 = (f32[256,2036]{0,1:T(8,128)}, f32[256,2036]{0,1:T(8,128)}) fusion(f32[256,2048]{0,1:T(8,128)S(1)} %bitcast.55), kind=kLoop, calls=%fused_computation.111 | loop fusion | bytes 8339456 | tf_op jit(solution)/shard_map/jit(_roll_static)/slice | solution.py:49
  51.8 2.3 %fusion.68 = (f32[256,2037]{0,1:T(8,128)}, f32[256,2037]{0,1:T(8,128)}) fusion(f32[256,2048]{0,1:T(8,128)S(1)} %bitcast.56), kind=kLoop, calls=%fused_computation.113 | loop fusion | bytes 8343552 | tf_op jit(solution)/shard_map/jit(_roll_static)/slice | solution.py:49
  54.1 2.3 %fusion.70 = (f32[256,2038]{0,1:T(8,128)}, f32[256,2038]{0,1:T(8,128)}) fusion(f32[256,2048]{0,1:T(8,128)S(1)} %bitcast.57), kind=kLoop, calls=%fused_computation.115 | loop fusion | bytes 8347648 | tf_op jit(solution)/shard_map/jit(_roll_static)/slice | solution.py:49
  56.3 2.3 %fusion.72 = (f32[256,2039]{0,1:T(8,128)}, f32[256,2039]{0,1:T(8,128)}) fusion(f32[256,2048]{0,1:T(8,128)S(1)} %bitcast.58), kind=kLoop, calls=%fused_computation.117 | loop fusion | bytes 8351744 | tf_op jit(solution)/shard_map/jit(_roll_static)/slice | solution.py:49
  58.6 2.2 %fusion.74 = (f32[256,2040]{0,1:T(8,128)}, f32[256,2040]{0,1:T(8,128)}) fusion(f32[256,2048]{0,1:T(8,128)S(1)} %bitcast.59), kind=kLoop, calls=%fused_computation.119 | loop fusion | bytes 8355840 | tf_op jit(solution)/shard_map/jit(_roll_static)/slice | solution.py:49
  60.8 2.3 %fusion.60 = (f32[256,2033]{0,1:T(8,128)}, f32[256,2033]{0,1:T(8,128)}) fusion(f32[256,2048]{0,1:T(8,128)S(1)} %bitcast.60), kind=kLoop, calls=%fused_computation.105 | loop fusion | bytes 8327168 | tf_op jit(solution)/shard_map/jit(_roll_static)/slice | solution.py:49
  63.3 27.8 %fusion.40 = f32[256,1024]{1,0:T(8,128)S(1)} fusion(bf16[2048,1024]{1,0:T(8,128)(2,1)} %constant.58.clone, f32[256,2038]{0,1:T(8,128)} %get-tuple-element.26, f32[256,10]{0,1:T(8,128)S(1)} %get-tuple-element.28, f32[256,2037]{0,1:T(8,128)} %get-tuple-element.22, f32[256,11]{0,1:T(8,128)S(1)} %get-tuple-element.24, f32[256,2036]{0,1:T(8,128)} %get-tuple-element.18, ...), kind=kOutput, calls=%fused_computation.74 | convolution fusion | flops 1121976320 | bytes 70254592 | tf_op jit(solution)/shard_map/dot_general | solution.py:68
  91.1 0.1 multiply_add_fusion
  91.2 0.2 copy.22
  91.6 0.2 copy.23
  91.8 0.0 copy-start
  91.8 0.0 copy-start.1
  91.8 0.2 multiply_convert_fusion
  92.0 0.9 pad_maximum_fusion
  92.9 0.0 all-gather.2.cloned.1.call-update
  93.0 0.0 copy-done
  93.0 11.8 %all_gather.7 = bf16[4,1,4,1]{2,3,1,0:T(2,128)(2,1)S(1)} all-gather(bf16[1,1,4,1]{2,3,1,0:T(2,128)(2,1)S(1)} %convert_element_type.49), channel_id=1, replica_groups=mesh['groups'=2,'chan'=4,'tm'=4] {'chan'}, dimensions={0}, use_global_device_ids=true | all-gather | bytes 40 | tf_op jit(solution)/shard_map/all_gather | solution.py:75
  104.8 0.2 convert_reduce_fusion
  105.1 0.0 copy-done.1
  105.1 35.0 %all-gather.2.cloned.1.call-done = bf16[8,128,1024]{2,1,0:T(8,128)(2,1)} async-done(((bf16[2,128,1024]{2,1,0:T(8,128)(2,1)}), bf16[8,128,1024]{2,1,0:T(8,128)(2,1)}) %all-gather.2.cloned.1.call-update) | async-done | bytes 2097168 | tf_op jit(solution)/shard_map/all_gather | solution.py:74
  140.1 2.2 %gather_fusion = bf16[4,128,1024]{2,1,0:T(8,128)(2,1)S(1)} fusion(bf16[8,128,1024]{2,1,0:T(8,128)(2,1)} %all-gather.2.cloned.1.call-done, s32[1024]{0:T(1024)S(1)} %pad_clamp_fusion), kind=kCustom, calls=%fused_computation | custom fusion | bytes 2097168 | tf_op jit(solution)/shard_map/gather | solution.py:80
  142.3 0.8 fusion.34
  143.1 1.0 copy.27
  (23 shorter events, 0.2 us)
Async XLA Ops:
  6.5 133.6 %all-gather.2.cloned.1.call-start = ((), (), s32[]{:S(2)}) async-start(), calls=%async_computation.1 | async-start | bytes 2621440 | tf_op jit(solution)/shard_map/all_gather | solution.py:74
  91.8 1.2 copy-start
  91.8 13.3 %copy-start.1 = (s32[1,1,4]{2,1,0:T(1,128)S(1)}, s32[1,1,4]{2,1,0:T(1,128)}, u32[]{:S(2)}) copy-start(s32[1,1,4]{2,1,0:T(1,128)} %param.6) | copy-start | bytes 52
Sparse Core Ops, SparseCore 0:
  93.1 46.9 all-gather.1
where the time goes:
time: 151 us
  local copies, waits for them, and re-layouts  40 us (26%)
  waiting for transfers between devices  35 us (23%)
  blocking collectives  30.5 us (20%)
  matrix products  28.6 us (19%)
  between operations  13.7 us (9%)
  other arithmetic  3.18 us (2%)
    all_gather x1, waiting for transfers between devices, local(): lax.all_gather(whitened, 'chan', axis=0, tiled=True)  35 us
    slice x30, local copies, waits for them, and re-layouts, band_filter(): jnp.roll(signal, index - RAD, axis=1)  34.4 us
    dot_general x1, matrix products, local(): jnp.dot(band_filter(rows), table, preferred_element_type=jnp.float32)  27.8 us
    all_to_all x1, blocking collectives, local(): rows = lax.all_to_all(raw, 'tm', split_axis=0, concat_axis=1, tiled=True)  18.7 us
    all_gather x1, blocking collectives, local(): lax.all_gather(send_blocks.astype(jnp.bfloat16), 'chan', axis=0, tiled=True)  11.8 us
  transfers between devices with their start and end apart: 1, of which 1 were waited for; matrix products, arithmetic and copies ran while one was open for 0% of the time, Pallas kernels for 0%

commit v1 on v0

v1 whole, which is shorter than its diff:
```python
import functools
import math

import jax
import jax.numpy as jnp
import numpy as np
from jax import lax
from jax.experimental import pallas as pl
from jax.experimental.pallas import tpu as pltpu
from jax.sharding import PartitionSpec as P

BLOCK = 128
NT = 2048
F0 = 128
NBAND = 512
SUBW = 64
RAD = 15
TILE = 256
SIDE = 128


def sinc_value(arg):
    if arg == 0:
        return 1.0
    return math.sin(math.pi * arg) / (math.pi * arg)


def filter_taps():
    low = F0 / NT
    high = (F0 + NBAND) / NT
    taps = []
    for offset in range(-RAD, RAD + 1):
        value = 2.0 * high * sinc_value(2.0 * high * offset) - 2.0 * low * sinc_value(
            2.0 * low * offset
        )
        value = value * (0.5 + 0.5 * math.cos(math.pi * offset / (RAD + 1)))
        taps.append(value)
    return taps


def dft_table():
    samples = np.arange(NT)[:, None]
    freqs = np.arange(F0, F0 + NBAND)[None, :]
    phase = samples * freqs % NT
    angle = 2.0 * np.pi * phase / NT
    return np.concatenate([np.cos(angle), -np.sin(angle)], axis=1)


def filter_bands():
    taps = np.asarray(filter_taps(), np.float64).astype(np.float32)
    u = np.arange(TILE + 2 * SIDE)[:, None]
    v = np.arange(TILE)[None, :]
    k = v + SIDE - u
    band = np.where(np.abs(k) <= RAD, taps[np.clip(k + RAD, 0, 2 * RAD)], 0).astype(np.float32)
    first = band.astype(jnp.bfloat16)
    second = (band - first.astype(np.float32)).astype(jnp.bfloat16)
    return np.stack([first, second])


def segment_ones():
    run = np.arange(128) // SUBW
    return (run[:, None] == run[None, :]).astype(jnp.bfloat16)


def dot(a, b):
    return jnp.dot(a, b, preferred_element_type=jnp.float32)


def kernel(
    peers,
    teams,
    raw_ref,
    table_ref,
    bands_ref,
    ones_ref,
    send_ref,
    count_ref,
    out_ref,
    rows,
    table,
    filtered,
    paired,
    outbox,
    inbox,
    table_sem,
    own_sem,
    tm_send,
    tm_recv,
    ch_send,
    ch_recv,
):
    c = lax.axis_index("chan")
    t = lax.axis_index("tm")
    blocks = rows.shape[0]
    span = raw_ref.shape[1]

    load_table = pltpu.make_async_copy(table_ref, table, table_sem)
    load_table.start()

    barrier = pltpu.get_barrier_semaphore()
    for o in range(1, teams):
        pl.semaphore_signal(barrier, inc=1, device_id={"tm": lax.rem(t + o, teams)})
    for o in range(1, peers):
        pl.semaphore_signal(barrier, inc=1, device_id={"chan": lax.rem(c + o, peers)})
    pl.semaphore_wait(barrier, teams + peers - 2)

    mine = pl.ds(pl.multiple_of(t * span, 128), span)

    def part(o, l):
        q = lax.rem(t + o, teams)
        start = pl.multiple_of((q * blocks + l) * BLOCK, BLOCK)
        return pltpu.make_async_remote_copy(
            src_ref=raw_ref.at[pl.ds(start, BLOCK), :],
            dst_ref=rows.at[l, :, mine],
            send_sem=tm_send.at[o - 1, l],
            recv_sem=tm_recv.at[o - 1, l],
            device_id={"tm": q},
        )

    def own(l):
        start = pl.multiple_of((t * blocks + l) * BLOCK, BLOCK)
        return pltpu.make_async_copy(
            raw_ref.at[pl.ds(start, BLOCK), :], rows.at[l, :, mine], own_sem.at[l]
        )

    for l in range(blocks):
        for o in range(1, teams):
            part(o, l).start()
        own(l).start()
    load_table.wait()

    def block_step(l, carry):
        own(l).wait()
        for o in range(1, teams):
            part(o, l).wait_recv()
        for j in range(NT // TILE):
            lo, hi = j * TILE - SIDE, (j + 1) * TILE + SIDE
            if lo < 0:
                window = jnp.concatenate([rows[l, :, NT + lo :], rows[l, :, :hi]], axis=1)
            elif hi > NT:
                window = jnp.concatenate([rows[l, :, lo:], rows[l, :, : hi - NT]], axis=1)
            else:
                window = rows[l, :, lo:hi]
            value = dot(window, bands_ref[0]) + dot(window, bands_ref[1])
            filtered[:, j * TILE : (j + 1) * TILE] = value.astype(jnp.bfloat16)
        step = 256
        for f in range(0, NBAND, step):
            real = dot(filtered[...], table[:, f : f + step])
            imag = dot(filtered[...], table[:, NBAND + f : NBAND + f + step])
            power = real * real + imag * imag
            for g in range(0, step, 128):
                p = power[:, g : g + 128]
                first = p.astype(jnp.bfloat16)
                second = (p - first.astype(jnp.float32)).astype(jnp.bfloat16)
                total = dot(first, ones_ref[...]) + dot(second, ones_ref[...])
                level = lax.rsqrt(total * (1.0 / SUBW) + 1e-06)
                re = (real[:, g : g + 128] * level).astype(jnp.bfloat16)
                im = (imag[:, g : g + 128] * level).astype(jnp.bfloat16)
                at = f + g
                paired[l, 0, :, at : at + 128] = re
                paired[l, 0, :, NBAND + at : NBAND + at + 128] = im
                paired[l, 1, :, at : at + 128] = im
                paired[l, 1, :, NBAND + at : NBAND + at + 128] = -re
        return carry

    lax.fori_loop(0, blocks, block_step, 0)

    def send(o):
        d = lax.rem(c + o, peers)
        return pltpu.make_async_remote_copy(
            src_ref=outbox.at[o - 1],
            dst_ref=inbox.at[o - 1],
            send_sem=ch_send.at[o - 1],
            recv_sem=ch_recv.at[o - 1],
            device_id={"chan": d},
        )

    for o in range(1, peers):
        d = lax.rem(c + o, peers)
        outbox[o - 1] = paired[send_ref[0, 0, d, 0], 0]
        send(o).start()

    out_ref[0, 0, c] = jnp.zeros(out_ref.shape[3:], out_ref.dtype)
    flat = paired.shape[0] * paired.shape[1] * BLOCK
    for o in range(1, peers):
        p = lax.rem(c - o + peers, peers)
        send(o).wait_recv()
        left = paired[...].reshape(flat, 2 * NBAND)
        value = lax.dot_general(
            left, inbox[o - 1], (((1,), (1,)), ((), ())), preferred_element_type=jnp.float32
        )
        value = value * (1.0 / math.sqrt(NBAND))
        value = jnp.where(count_ref[0, 0, p] > 0, value, 0.0)
        out_ref[0, 0, p] = value.astype(out_ref.dtype).reshape(out_ref.shape[3:])

    for l in range(blocks):
        for o in range(1, teams):
            part(o, l).wait_send()
    for o in range(1, peers):
        send(o).wait_send()


def local(peers, teams, raw, send_blocks, pair_count):
    table = jnp.asarray(dft_table(), dtype=jnp.bfloat16)
    bands = jnp.asarray(filter_bands())
    ones = jnp.asarray(segment_ones())
    blocks = raw.shape[0] // (teams * BLOCK)
    vmem = pl.BlockSpec(memory_space=pltpu.VMEM)
    smem = pl.BlockSpec(memory_space=pltpu.SMEM)
    anywhere = pl.BlockSpec(memory_space=pl.ANY)
    return pl.pallas_call(
        functools.partial(kernel, peers, teams),
        out_shape=jax.ShapeDtypeStruct((1, 1, peers, 1, blocks, 2, BLOCK, BLOCK), jnp.bfloat16),
        in_specs=[anywhere, anywhere, vmem, vmem, smem, smem],
        out_specs=vmem,
        scratch_shapes=[
            pltpu.VMEM((blocks, BLOCK, NT), jnp.bfloat16),
            pltpu.VMEM((NT, 2 * NBAND), jnp.bfloat16),
            pltpu.VMEM((BLOCK, NT), jnp.bfloat16),
            pltpu.VMEM((blocks, 2, BLOCK, 2 * NBAND), jnp.bfloat16),
            pltpu.VMEM((peers - 1, BLOCK, 2 * NBAND), jnp.bfloat16),
            pltpu.VMEM((peers - 1, BLOCK, 2 * NBAND), jnp.bfloat16),
            pltpu.SemaphoreType.DMA,
            pltpu.SemaphoreType.DMA((blocks,)),
            pltpu.SemaphoreType.DMA((teams - 1, blocks)),
            pltpu.SemaphoreType.DMA((teams - 1, blocks)),
            pltpu.SemaphoreType.DMA((peers - 1,)),
            pltpu.SemaphoreType.DMA((peers - 1,)),
        ],
        compiler_params=pltpu.CompilerParams(
            collective_id=0, has_side_effects=True, vmem_limit_bytes=48 * 1024 * 1024
        ),
        cost_estimate=pl.CostEstimate(
            flops=3_000_000_000, bytes_accessed=6_000_000, transcendentals=0
        ),
    )(raw, table, bands, ones, send_blocks, pair_count)


def solution(mesh):
    return jax.shard_map(
        functools.partial(local, mesh.shape["chan"], mesh.shape["tm"]),
        mesh=mesh,
        in_specs=(P(("groups", "chan"), "tm"), P("chan", "tm", None, None), P("chan", "tm", None)),
        out_specs=P(("groups", "chan"), "tm", None, None, None, None, None, None),
        check_vma=False,
    )
```

time: 151 us -> 47.8 us (0.32)
  the two profiles are of different devices: /device:TPU:0 before, /device:TPU:29 now
where the time goes in v1:
time: 47.8 us; the launch traced here: 47.5 us
  Pallas kernels  42.3 us (88%)
  local copies, waits for them, and re-layouts  5.21 us (11%)
    pallas_call x1, Pallas kernels, local(): pl.pallas_call(functools.partial(kernel, peers, teams), out_shape=jax.Sha...  42.3 us
    unnamed x10, local copies, waits for them, and re-layouts  5.21 us

profile of v1, /device:TPU:29, one launch (start us, length us, event | category | flops | bytes accessed | tf_op | source)
XLA Modules:
  0.0 47.5 jit_solution(5913400428012047643)
XLA Ops:
  0.0 0.7 %copy.7.send_ref = s32[1,1,4,1]{3,2,1,0:T(4,128)S(1)} copy(s32[1,1,4,1]{2,3,1,0:T(1,128)} %param.7) | data formatting | bytes 32 | tf_op args[1]
  0.7 0.0 copy-start
  0.7 1.2 %copy-done = bf16[1024,512]{1,0:T(8,128)(2,1)S(1)} copy-done((bf16[1024,512]{1,0:T(8,128)(2,1)S(1)}, bf16[1024,512]{1,0:T(8,128)(2,1)}, u32[]{:S(2)}) %copy-start) | copy-done | bytes 1048600
  2.0 0.0 copy-start.1
  2.0 0.7 %copy-done.1 = s32[1,1,4]{2,1,0:T(1,128)S(1)} copy-done((s32[1,1,4]{2,1,0:T(1,128)S(1)}, s32[1,1,4]{2,1,0:T(1,128)}, u32[]{:S(2)}) %copy-start.1) | copy-done | bytes 40
  2.6 0.0 copy-start.2
  2.6 1.0 %copy-done.2 = bf16[2,512,256]{2,1,0:T(8,128)(2,1)S(1)} copy-done((bf16[2,512,256]{2,1,0:T(8,128)(2,1)S(1)}, bf16[2,512,256]{2,1,0:T(8,128)(2,1)}, u32[]{:S(2)}) %copy-start.2) | copy-done | bytes 524312
  3.7 0.0 copy-start.3
  3.7 0.8 %copy-done.3 = bf16[128,128]{1,0:T(8,128)(2,1)S(1)} copy-done((bf16[128,128]{1,0:T(8,128)(2,1)S(1)}, bf16[128,128]{1,0:T(8,128)(2,1)}, u32[]{:S(2)}) %copy-start.3) | copy-done | bytes 32792
  4.4 42.3 %shard_map.64 = bf16[1,1,4,1,2,2,128,128]{7,6,5,4,3,2,1,0:T(8,128)(2,1)S(1)} custom-call(bf16[1024,512]{1,0:T(8,128)(2,1)S(1)} %copy-done, bf16[2048,1024]{1,0:T(8,128)(2,1)} %constant.6.clone.table_ref, bf16[2,512,256]{2,1,0:T(8,128)(2,1)S(1)} %copy-done.2, bf16[128,128]{1,0:T(8,128)(2,1)S(1)} %copy-done.3, s32[1,1,4,1]{3,2,1,0:T(4,128)S(1)} %copy.7.send_ref, ...), custom_call_target="tpu_custom_call" | custom-call | flops 3000000000 | bytes 6000000 | tf_op jit(solution)/shard_map/pallas_call | solution.py:211
  46.7 0.8 %copy.9 = bf16[1,1,4,1,2,2,128,128]{7,6,5,4,3,2,1,0:T(8,128)(2,1)} copy(bf16[1,1,4,1,2,2,128,128]{7,6,5,4,3,2,1,0:T(8,128)(2,1)S(1)} %shard_map.64) | data formatting | bytes 1048576
Async XLA Ops:
  0.7 1.2 %copy-start = (bf16[1024,512]{1,0:T(8,128)(2,1)S(1)}, bf16[1024,512]{1,0:T(8,128)(2,1)}, u32[]{:S(2)}) copy-start(bf16[1024,512]{1,0:T(8,128)(2,1)} %raw_ref.1) | copy-start | bytes 3145732
  2.0 0.7 %copy-start.1 = (s32[1,1,4]{2,1,0:T(1,128)S(1)}, s32[1,1,4]{2,1,0:T(1,128)}, u32[]{:S(2)}) copy-start(s32[1,1,4]{2,1,0:T(1,128)} %count_ref.1) | copy-start | bytes 52
  2.6 1.0 %copy-start.2 = (bf16[2,512,256]{2,1,0:T(8,128)(2,1)S(1)}, bf16[2,512,256]{2,1,0:T(8,128)(2,1)}, u32[]{:S(2)}) copy-start(bf16[2,512,256]{2,1,0:T(8,128)(2,1)} %constant.7.clone.bands_ref) | copy-start | bytes 1572868
  3.7 0.8 %copy-start.3 = (bf16[128,128]{1,0:T(8,128)(2,1)S(1)}, bf16[128,128]{1,0:T(8,128)(2,1)}, u32[]{:S(2)}) copy-start(bf16[128,128]{1,0:T(8,128)(2,1)} %constant.8.clone.ones_ref) | copy-start | bytes 98308

commit v2 on v1

--- a/solution.py
+++ b/solution.py
@@ -16,6 +16,8 @@
 SUBW = 64
 RAD = 15
 TILE = 256
+CHUNK = 128
+CHUNKS = NBAND // CHUNK
 SIDE = 128
 
 
@@ -78,11 +80,13 @@
     out_ref,
     rows,
     table,
+    bands,
+    ones,
     filtered,
     paired,
     outbox,
     inbox,
-    table_sem,
+    load_sem,
     own_sem,
     tm_send,
     tm_recv,
@@ -94,8 +98,13 @@
     blocks = rows.shape[0]
     span = raw_ref.shape[1]
 
-    load_table = pltpu.make_async_copy(table_ref, table, table_sem)
-    load_table.start()
+    loads = [
+        pltpu.make_async_copy(bands_ref, bands, load_sem.at[0]),
+        pltpu.make_async_copy(ones_ref, ones, load_sem.at[1]),
+        pltpu.make_async_copy(table_ref, table, load_sem.at[2]),
+    ]
+    for load in loads:
+        load.start()
 
     barrier = pltpu.get_barrier_semaphore()
     for o in range(1, teams):
@@ -127,9 +136,11 @@
         for o in range(1, teams):
             part(o, l).start()
         own(l).start()
-    load_table.wait()
-
-    def block_step(l, carry):
+    out_ref[0, 0, c] = jnp.zeros(out_ref.shape[3:], out_ref.dtype)
+    for load in loads:
+        load.wait()
+
+    def filter_block(l, carry):
         own(l).wait()
         for o in range(1, teams):
             part(o, l).wait_recv()
@@ -141,67 +152,68 @@
                 window = jnp.concatenate([rows[l, :, lo:], rows[l, :, : hi - NT]], axis=1)
             else:
                 window = rows[l, :, lo:hi]
-            value = dot(window, bands_ref[0]) + dot(window, bands_ref[1])
-            filtered[:, j * TILE : (j + 1) * TILE] = value.astype(jnp.bfloat16)
-        step = 256
-        for f in range(0, NBAND, step):
-            real = dot(filtered[...], table[:, f : f + step])
-            imag = dot(filtered[...], table[:, NBAND + f : NBAND + f + step])
-            power = real * real + imag * imag
-            for g in range(0, step, 128):
-                p = power[:, g : g + 128]
-                first = p.astype(jnp.bfloat16)
-                second = (p - first.astype(jnp.float32)).astype(jnp.bfloat16)
-                total = dot(first, ones_ref[...]) + dot(second, ones_ref[...])
-                level = lax.rsqrt(total * (1.0 / SUBW) + 1e-06)
-                re = (real[:, g : g + 128] * level).astype(jnp.bfloat16)
-                im = (imag[:, g : g + 128] * level).astype(jnp.bfloat16)
-                at = f + g
-                paired[l, 0, :, at : at + 128] = re
-                paired[l, 0, :, NBAND + at : NBAND + at + 128] = im
-                paired[l, 1, :, at : at + 128] = im
-                paired[l, 1, :, NBAND + at : NBAND + at + 128] = -re
+            value = dot(window, bands[0]) + dot(window, bands[1])
+            filtered[l, :, j * TILE : (j + 1) * TILE] = value.astype(jnp.bfloat16)
         return carry
 
-    lax.fori_loop(0, blocks, block_step, 0)
-
-    def send(o):
-        d = lax.rem(c + o, peers)
+    lax.fori_loop(0, blocks, filter_block, 0)
+
+    def send(o, k):
         return pltpu.make_async_remote_copy(
-            src_ref=outbox.at[o - 1],
-            dst_ref=inbox.at[o - 1],
-            send_sem=ch_send.at[o - 1],
-            recv_sem=ch_recv.at[o - 1],
-            device_id={"chan": d},
-        )
-
-    for o in range(1, peers):
-        d = lax.rem(c + o, peers)
-        outbox[o - 1] = paired[send_ref[0, 0, d, 0], 0]
-        send(o).start()
-
-    out_ref[0, 0, c] = jnp.zeros(out_ref.shape[3:], out_ref.dtype)
-    flat = paired.shape[0] * paired.shape[1] * BLOCK
+            src_ref=outbox.at[o - 1, k],
+            dst_ref=inbox.at[o - 1, k],
+            send_sem=ch_send.at[o - 1, k],
+            recv_sem=ch_recv.at[o - 1, k],
+            device_id={"chan": lax.rem(c + o, peers)},
+        )
+
+    for k in range(CHUNKS):
+        at = k * 2 * CHUNK
+        signal = filtered[...].reshape(blocks * BLOCK, NT)
+        value = dot(signal, table[:, at : at + 2 * CHUNK])
+        real, imag = value[:, :CHUNK], value[:, CHUNK:]
+        power = real * real + imag * imag
+        first = power.astype(jnp.bfloat16)
+        second = (power - first.astype(jnp.float32)).astype(jnp.bfloat16)
+        total = dot(first, ones[...]) + dot(second, ones[...])
+        level = lax.rsqrt(total * (1.0 / SUBW) + 1e-06)
+        re = (real * level).astype(jnp.bfloat16).reshape(blocks, BLOCK, CHUNK)
+        im = (imag * level).astype(jnp.bfloat16).reshape(blocks, BLOCK, CHUNK)
+        paired[k, :, 0, :, :CHUNK] = re
+        paired[k, :, 0, :, CHUNK:] = im
+        for o in range(1, peers):
+            outbox[o - 1, k] = paired[k, send_ref[lax.rem(c + o, peers)], 0]
+            send(o, k).start()
+        paired[k, :, 1, :, :CHUNK] = im
+        paired[k, :, 1, :, CHUNK:] = -re
+
+    flat = 2 * blocks * BLOCK
     for o in range(1, peers):
         p = lax.rem(c - o + peers, peers)
-        send(o).wait_recv()
-        left = paired[...].reshape(flat, 2 * NBAND)
-        value = lax.dot_general(
-            left, inbox[o - 1], (((1,), (1,)), ((), ())), preferred_element_type=jnp.float32
-        )
+        value = jnp.zeros((flat, BLOCK), jnp.float32)
+        for k in range(CHUNKS):
+            send(o, k).wait_recv()
+            value = value + lax.dot_general(
+                paired[k].reshape(flat, 2 * CHUNK),
+                inbox[o - 1, k],
+                (((1,), (1,)), ((), ())),
+                preferred_element_type=jnp.float32,
+            )
         value = value * (1.0 / math.sqrt(NBAND))
-        value = jnp.where(count_ref[0, 0, p] > 0, value, 0.0)
+        value = jnp.where(count_ref[p] > 0, value, 0.0)
         out_ref[0, 0, p] = value.astype(out_ref.dtype).reshape(out_ref.shape[3:])
 
     for l in range(blocks):
         for o in range(1, teams):
             part(o, l).wait_send()
     for o in range(1, peers):
-        send(o).wait_send()
+        for k in range(CHUNKS):
+            send(o, k).wait_send()
 
 
 def local(peers, teams, raw, send_blocks, pair_count):
-    table = jnp.asarray(dft_table(), dtype=jnp.bfloat16)
+    table = dft_table().reshape(NT, 2, CHUNKS, CHUNK).transpose(0, 2, 1, 3)
+    table = jnp.asarray(table.reshape(NT, 2 * NBAND), dtype=jnp.bfloat16)
     bands = jnp.asarray(filter_bands())
     ones = jnp.asarray(segment_ones())
     blocks = raw.shape[0] // (teams * BLOCK)
@@ -211,29 +223,31 @@
     return pl.pallas_call(
         functools.partial(kernel, peers, teams),
         out_shape=jax.ShapeDtypeStruct((1, 1, peers, 1, blocks, 2, BLOCK, BLOCK), jnp.bfloat16),
-        in_specs=[anywhere, anywhere, vmem, vmem, smem, smem],
+        in_specs=[anywhere, anywhere, anywhere, anywhere, smem, smem],
         out_specs=vmem,
         scratch_shapes=[
             pltpu.VMEM((blocks, BLOCK, NT), jnp.bfloat16),
-            pltpu.VMEM((NT, 2 * NBAND), jnp.bfloat16),
-            pltpu.VMEM((BLOCK, NT), jnp.bfloat16),
-            pltpu.VMEM((blocks, 2, BLOCK, 2 * NBAND), jnp.bfloat16),
-            pltpu.VMEM((peers - 1, BLOCK, 2 * NBAND), jnp.bfloat16),
-            pltpu.VMEM((peers - 1, BLOCK, 2 * NBAND), jnp.bfloat16),
-            pltpu.SemaphoreType.DMA,
+            pltpu.VMEM(table.shape, jnp.bfloat16),
+            pltpu.VMEM(bands.shape, jnp.bfloat16),
+            pltpu.VMEM(ones.shape, jnp.bfloat16),
+            pltpu.VMEM((blocks, BLOCK, NT), jnp.bfloat16),
+            pltpu.VMEM((CHUNKS, blocks, 2, BLOCK, 2 * CHUNK), jnp.bfloat16),
+            pltpu.VMEM((peers - 1, CHUNKS, BLOCK, 2 * CHUNK), jnp.bfloat16),
+            pltpu.VMEM((peers - 1, CHUNKS, BLOCK, 2 * CHUNK), jnp.bfloat16),
+            pltpu.SemaphoreType.DMA((3,)),
             pltpu.SemaphoreType.DMA((blocks,)),
             pltpu.SemaphoreType.DMA((teams - 1, blocks)),
             pltpu.SemaphoreType.DMA((teams - 1, blocks)),
-            pltpu.SemaphoreType.DMA((peers - 1,)),
-            pltpu.SemaphoreType.DMA((peers - 1,)),
+            pltpu.SemaphoreType.DMA((peers - 1, CHUNKS)),
+            pltpu.SemaphoreType.DMA((peers - 1, CHUNKS)),
         ],
         compiler_params=pltpu.CompilerParams(
-            collective_id=0, has_side_effects=True, vmem_limit_bytes=48 * 1024 * 1024
+            collective_id=0, has_side_effects=True, vmem_limit_bytes=62 * 1024 * 1024
         ),
         cost_estimate=pl.CostEstimate(
             flops=3_000_000_000, bytes_accessed=6_000_000, transcendentals=0
         ),
-    )(raw, table, bands, ones, send_blocks, pair_count)
+    )(raw, table, bands, ones, send_blocks.reshape(peers), pair_count.reshape(peers))
 
 
 def solution(mesh):

time: 47.8 us -> 46.4 us (0.971)
  the two profiles are of different devices: /device:TPU:29 before, /device:TPU:0 now
where the time goes in v2:
time: 46.4 us; the launch traced here: 46.3 us
  Pallas kernels  44.4 us (96%)
  local copies, waits for them, and re-layouts  1.89 us (4%)
    pallas_call x1, Pallas kernels, local(): pl.pallas_call(functools.partial(kernel, peers, teams), out_shape=jax.Sha...  44.4 us
    unnamed x1, local copies, waits for them, and re-layouts  1.89 us

profile of v2, /device:TPU:0, one launch (start us, length us, event | category | flops | bytes accessed | tf_op | source)
XLA Modules:
  0.0 46.3 jit_solution(17395042483806205432)
XLA Ops:
  0.0 44.4 %shard_map.64 = bf16[1,1,4,1,2,2,128,128]{7,6,5,4,3,2,1,0:T(8,128)(2,1)} custom-call(bf16[1024,512]{1,0:T(8,128)(2,1)} %raw_ref.1, bf16[2048,1024]{1,0:T(8,128)(2,1)} %constant.6.clone.table_ref, bf16[2,512,256]{2,1,0:T(8,128)(2,1)} %constant.7.clone.bands_ref, bf16[128,128]{1,0:T(8,128)(2,1)} %constant.8.clone.ones_ref, s32[4]{0:T(128)} %bitcast.2, s32[4]{0:T(128)} %bitcast.3), custom_call_target="tpu_custom_call" | custom-call | flops 3000000000 | bytes 6000000 | tf_op jit(solution)/shard_map/pallas_call | solution.py:223
  44.4 1.9 %copy.8 = bf16[1,1,4,1,2,2,128,128]{7,6,5,4,3,2,1,0:T(8,128)(2,1)} copy(bf16[1,1,4,1,2,2,128,128]{7,6,5,4,3,2,1,0:T(8,128)(2,1)} %shard_map.64) | data formatting | bytes 1048576

commit v3 on v2

--- a/solution.py
+++ b/solution.py
@@ -92,11 +92,41 @@
     tm_recv,
     ch_send,
     ch_recv,
+    choices,
+    chosen,
+    crossed,
+    handed,
+    choice_sem,
+    cross_send,
+    cross_recv,
+    hand_send,
 ):
     c = lax.axis_index("chan")
     t = lax.axis_index("tm")
     blocks = rows.shape[0]
     span = raw_ref.shape[1]
+
+    relay = peers == 4 and blocks == 2
+    inner = jnp.logical_and(relay, jnp.logical_and(c > 0, c < 3))
+    partner = 3 - c
+
+    def direct(o):
+        return jnp.logical_or(jnp.logical_not(inner), o == 5 - 2 * c)
+
+    def arrives(o):
+        return jnp.logical_or(jnp.logical_not(inner), o != 5 - 2 * c)
+
+    def put(slot, k, value):
+        inbox[slot, k] = value
+
+    def choice():
+        return pltpu.make_async_remote_copy(
+            src_ref=choices,
+            dst_ref=chosen,
+            send_sem=choice_sem.at[0],
+            recv_sem=choice_sem.at[1],
+            device_id={"chan": partner},
+        )
 
     loads = [
         pltpu.make_async_copy(bands_ref, bands, load_sem.at[0]),
@@ -136,11 +166,19 @@
         for o in range(1, teams):
             part(o, l).start()
         own(l).start()
+    if relay:
+
+        @pl.when(inner)
+        def _():
+            choices[0] = jnp.full((8, 128), send_ref[partner], jnp.int32)
+            choices[1] = jnp.full((8, 128), send_ref[6 - 3 * c], jnp.int32)
+            choice().start()
+
     out_ref[0, 0, c] = jnp.zeros(out_ref.shape[3:], out_ref.dtype)
     for load in loads:
         load.wait()
 
-    def filter_block(l, carry):
+    def filter_block(l):
         own(l).wait()
         for o in range(1, teams):
             part(o, l).wait_recv()
@@ -154,45 +192,88 @@
                 window = rows[l, :, lo:hi]
             value = dot(window, bands[0]) + dot(window, bands[1])
             filtered[l, :, j * TILE : (j + 1) * TILE] = value.astype(jnp.bfloat16)
-        return carry
-
-    lax.fori_loop(0, blocks, filter_block, 0)
-
-    def send(o, k):
-        return pltpu.make_async_remote_copy(
-            src_ref=outbox.at[o - 1, k],
-            dst_ref=inbox.at[o - 1, k],
-            send_sem=ch_send.at[o - 1, k],
-            recv_sem=ch_recv.at[o - 1, k],
-            device_id={"chan": lax.rem(c + o, peers)},
-        )
-
-    for k in range(CHUNKS):
+
+    def whiten_chunk(l, k):
         at = k * 2 * CHUNK
-        signal = filtered[...].reshape(blocks * BLOCK, NT)
-        value = dot(signal, table[:, at : at + 2 * CHUNK])
+        value = dot(filtered[l], table[:, at : at + 2 * CHUNK])
         real, imag = value[:, :CHUNK], value[:, CHUNK:]
         power = real * real + imag * imag
         first = power.astype(jnp.bfloat16)
         second = (power - first.astype(jnp.float32)).astype(jnp.bfloat16)
         total = dot(first, ones[...]) + dot(second, ones[...])
         level = lax.rsqrt(total * (1.0 / SUBW) + 1e-06)
-        re = (real * level).astype(jnp.bfloat16).reshape(blocks, BLOCK, CHUNK)
-        im = (imag * level).astype(jnp.bfloat16).reshape(blocks, BLOCK, CHUNK)
-        paired[k, :, 0, :, :CHUNK] = re
-        paired[k, :, 0, :, CHUNK:] = im
-        for o in range(1, peers):
-            outbox[o - 1, k] = paired[k, send_ref[lax.rem(c + o, peers)], 0]
-            send(o, k).start()
-        paired[k, :, 1, :, :CHUNK] = im
-        paired[k, :, 1, :, CHUNK:] = -re
+        re = (real * level).astype(jnp.bfloat16)
+        im = (imag * level).astype(jnp.bfloat16)
+        paired[k, l, 0, :, :CHUNK] = re
+        paired[k, l, 0, :, CHUNK:] = im
+        paired[k, l, 1, :, :CHUNK] = im
+        paired[k, l, 1, :, CHUNK:] = -re
+
+    def send(o, k):
+        return pltpu.make_async_remote_copy(
+            src_ref=outbox.at[o - 1, k],
+            dst_ref=inbox.at[o - 1, k],
+            send_sem=ch_send.at[o - 1, k],
+            recv_sem=ch_recv.at[o - 1, k],
+            device_id={"chan": lax.rem(c + o, peers)},
+        )
+
+    def cross(l, k):
+        return pltpu.make_async_remote_copy(
+            src_ref=paired.at[k, l, 0],
+            dst_ref=crossed.at[l, k],
+            send_sem=cross_send.at[l, k],
+            recv_sem=cross_recv.at[l, k],
+            device_id={"chan": partner},
+        )
+
+    def hand_on(k):
+        return pltpu.make_async_remote_copy(
+            src_ref=handed.at[k],
+            dst_ref=inbox.at[1, k],
+            send_sem=hand_send.at[k],
+            recv_sem=ch_recv.at[1, k],
+            device_id={"chan": 3 * (c - 1)},
+        )
+
+    def start_send(o, k):
+        outbox[o - 1, k] = paired[k, send_ref[lax.rem(c + o, peers)], 0]
+        send(o, k).start()
+
+    for l in range(blocks):
+        filter_block(l)
+        for k in range(CHUNKS):
+            whiten_chunk(l, k)
+            if relay:
+                pl.when(inner)(lambda l=l, k=k: cross(l, k).start())
+            if l == blocks - 1:
+                for o in range(1, peers):
+                    pl.when(direct(o))(lambda o=o, k=k: start_send(o, k))
+
+    if relay:
+
+        @pl.when(inner)
+        def _():
+            choice().wait_recv()
+            for_me = jnp.concatenate([chosen[0, :1], chosen[0, :1]], axis=1) > 0
+            for_next = jnp.concatenate([chosen[1, :1], chosen[1, :1]], axis=1) > 0
+            for k in range(CHUNKS):
+                for l in range(blocks):
+                    cross(l, k).wait_recv()
+                zero = crossed[0, k].astype(jnp.float32)
+                one = crossed[1, k].astype(jnp.float32)
+                handed[k] = jnp.where(for_next, one, zero).astype(jnp.bfloat16)
+                hand_on(k).start()
+                mine_now = jnp.where(for_me, one, zero).astype(jnp.bfloat16)
+                pl.when(c == 1)(lambda k=k, v=mine_now: put(2, k, v))
+                pl.when(c == 2)(lambda k=k, v=mine_now: put(0, k, v))
 
     flat = 2 * blocks * BLOCK
     for o in range(1, peers):
         p = lax.rem(c - o + peers, peers)
         value = jnp.zeros((flat, BLOCK), jnp.float32)
         for k in range(CHUNKS):
-            send(o, k).wait_recv()
+            pl.when(arrives(o))(lambda o=o, k=k: send(o, k).wait_recv())
             value = value + lax.dot_general(
                 paired[k].reshape(flat, 2 * CHUNK),
                 inbox[o - 1, k],
@@ -208,7 +289,16 @@
             part(o, l).wait_send()
     for o in range(1, peers):
         for k in range(CHUNKS):
-            send(o, k).wait_send()
+            pl.when(direct(o))(lambda o=o, k=k: send(o, k).wait_send())
+    if relay:
+
+        @pl.when(inner)
+        def _():
+            choice().wait_send()
+            for k in range(CHUNKS):
+                hand_on(k).wait_send()
+                for l in range(blocks):
+                    cross(l, k).wait_send()
 
 
 def local(peers, teams, raw, send_blocks, pair_count):
@@ -240,6 +330,14 @@
             pltpu.SemaphoreType.DMA((teams - 1, blocks)),
             pltpu.SemaphoreType.DMA((peers - 1, CHUNKS)),
             pltpu.SemaphoreType.DMA((peers - 1, CHUNKS)),
+            pltpu.VMEM((2, 8, 128), jnp.int32),
+            pltpu.VMEM((2, 8, 128), jnp.int32),
+            pltpu.VMEM((blocks, CHUNKS, BLOCK, 2 * CHUNK), jnp.bfloat16),
+            pltpu.VMEM((CHUNKS, BLOCK, 2 * CHUNK), jnp.bfloat16),
+            pltpu.SemaphoreType.DMA((2,)),
+            pltpu.SemaphoreType.DMA((blocks, CHUNKS)),
+            pltpu.SemaphoreType.DMA((blocks, CHUNKS)),
+            pltpu.SemaphoreType.DMA((CHUNKS,)),
         ],
         compiler_params=pltpu.CompilerParams(
             collective_id=0, has_side_effects=True, vmem_limit_bytes=62 * 1024 * 1024

time: 46.4 us -> 45 us (0.970)
  Pallas kernels: 44.4 us -> 42.9 us
    pallas_call x1, Pallas kernels: 44.4 us -> 42.9 us  [local(): pl.pallas_call(functools.partial(kernel, peers, teams), out_shape=jax.Sha...]
where the time goes in v3:
time: 45 us; the launch traced here: 44.8 us
  Pallas kernels  42.9 us (95%)
  local copies, waits for them, and re-layouts  1.89 us (4%)
    pallas_call x1, Pallas kernels, local(): pl.pallas_call(functools.partial(kernel, peers, teams), out_shape=jax.Sha...  42.9 us
    unnamed x1, local copies, waits for them, and re-layouts  1.89 us

profile of v3, /device:TPU:0, one launch (start us, length us, event | category | flops | bytes accessed | tf_op | source)
XLA Modules:
  0.0 44.8 jit_solution(13183305739626122687)
XLA Ops:
  0.0 42.9 %shard_map.64 = bf16[1,1,4,1,2,2,128,128]{7,6,5,4,3,2,1,0:T(8,128)(2,1)} custom-call(bf16[1024,512]{1,0:T(8,128)(2,1)} %raw_ref.1, bf16[2048,1024]{1,0:T(8,128)(2,1)} %constant.6.clone.table_ref, bf16[2,512,256]{2,1,0:T(8,128)(2,1)} %constant.7.clone.bands_ref, bf16[128,128]{1,0:T(8,128)(2,1)} %constant.8.clone.ones_ref, s32[4]{0:T(128)} %bitcast.2, s32[4]{0:T(128)} %bitcast.3), custom_call_target="tpu_custom_call" | custom-call | flops 3000000000 | bytes 6000000 | tf_op jit(solution)/shard_map/pallas_call | solution.py:313
  43.0 1.9 %copy.8 = bf16[1,1,4,1,2,2,128,128]{7,6,5,4,3,2,1,0:T(8,128)(2,1)} copy(bf16[1,1,4,1,2,2,128,128]{7,6,5,4,3,2,1,0:T(8,128)(2,1)} %shard_map.64) | data formatting | bytes 1048576

commit v4 on v3

--- a/solution.py
+++ b/solution.py
@@ -76,7 +76,6 @@
     bands_ref,
     ones_ref,
     send_ref,
-    count_ref,
     out_ref,
     rows,
     table,
@@ -281,7 +280,6 @@
                 preferred_element_type=jnp.float32,
             )
         value = value * (1.0 / math.sqrt(NBAND))
-        value = jnp.where(count_ref[p] > 0, value, 0.0)
         out_ref[0, 0, p] = value.astype(out_ref.dtype).reshape(out_ref.shape[3:])
 
     for l in range(blocks):
@@ -310,10 +308,10 @@
     vmem = pl.BlockSpec(memory_space=pltpu.VMEM)
     smem = pl.BlockSpec(memory_space=pltpu.SMEM)
     anywhere = pl.BlockSpec(memory_space=pl.ANY)
-    return pl.pallas_call(
+    result = pl.pallas_call(
         functools.partial(kernel, peers, teams),
         out_shape=jax.ShapeDtypeStruct((1, 1, peers, 1, blocks, 2, BLOCK, BLOCK), jnp.bfloat16),
-        in_specs=[anywhere, anywhere, anywhere, anywhere, smem, smem],
+        in_specs=[anywhere, anywhere, anywhere, anywhere, smem],
         out_specs=vmem,
         scratch_shapes=[
             pltpu.VMEM((blocks, BLOCK, NT), jnp.bfloat16),
@@ -345,7 +343,9 @@
         cost_estimate=pl.CostEstimate(
             flops=3_000_000_000, bytes_accessed=6_000_000, transcendentals=0
         ),
-    )(raw, table, bands, ones, send_blocks.reshape(peers), pair_count.reshape(peers))
+    )(raw, table, bands, ones, send_blocks.reshape(peers))
+    live = pair_count[:, :, :, None, None, None, None, None] > 0
+    return jnp.where(live, result, jnp.bfloat16(0.0))
 
 
 def solution(mesh):

time: 45 us -> 45.7 us (1.016)
  other arithmetic: 0 us -> 2.6 us
  local copies, waits for them, and re-layouts: 1.89 us -> 0 us
    select_n x0 -> x1, other arithmetic: none -> 1.94 us  [local(): return jnp.where(live, result, jnp.bfloat16(0.0))]
    unnamed x1 -> x0, local copies, waits for them, and re-layouts: 1.89 us -> none
    gt x0 -> x1, other arithmetic: none -> 0.66 us  [local(): live = pair_count[:, :, :, None, None, None, None, None] > 0]
where the time goes in v4:
time: 45.7 us; the launch traced here: 45.5 us
  Pallas kernels  42.9 us (94%)
  other arithmetic  2.6 us (6%)
    pallas_call x1, Pallas kernels, local(): pl.pallas_call(functools.partial(kernel, peers, teams), out_shape=jax.Sha...  42.9 us
    select_n x1, other arithmetic, local(): return jnp.where(live, result, jnp.bfloat16(0.0))  1.94 us

profile of v4, /device:TPU:0, one launch (start us, length us, event | category | flops | bytes accessed | tf_op | source)
XLA Modules:
  0.0 45.5 jit_solution(13498809175167774951)
XLA Ops:
  0.0 0.7 %compare_bitcast_fusion = pred[4]{0:T(512)(128)(4,1)S(1)} fusion(s32[1,1,4]{2,1,0:T(1,128)} %param.8), kind=kLoop, calls=%fused_computation.1 | loop fusion | flops 4 | bytes 20 | tf_op jit(solution)/shard_map/gt | solution.py:347
  0.7 42.9 %shard_map.64 = bf16[1,1,4,1,2,2,128,128]{7,6,5,4,3,2,1,0:T(8,128)(2,1)} custom-call(bf16[1024,512]{1,0:T(8,128)(2,1)} %raw_ref.1, bf16[2048,1024]{1,0:T(8,128)(2,1)} %constant.10.clone.table_ref, bf16[2,512,256]{2,1,0:T(8,128)(2,1)} %constant.11.clone.bands_ref, bf16[128,128]{1,0:T(8,128)(2,1)} %constant.12.clone.ones_ref, s32[4]{0:T(128)} %bitcast.3), custom_call_target="tpu_custom_call" | custom-call | flops 3000000000 | bytes 6000000 | tf_op jit(solution)/shard_map/pallas_call | solution.py:311
  43.6 1.9 %broadcast_select_fusion = bf16[1,1,4,1,2,2,128,128]{7,6,5,4,3,2,1,0:T(8,128)(2,1)} fusion(bf16[1,1,4,1,2,2,128,128]{7,6,5,4,3,2,1,0:T(8,128)(2,1)} %shard_map.64, pred[4]{0:T(512)(128)(4,1)S(1)} %compare_bitcast_fusion), kind=kLoop, calls=%fused_computation | loop fusion | flops 262144 | bytes 1048580 | tf_op jit(solution)/shard_map/jit(_where)/select_n | solution.py:348
